TPU v7x, 32 devices: a whole 2x2x4 slice. The times are simulated.
32 devices in a mesh: ha: 2 (over y), wa: 16 (over z, x, core).
Axes of the slice: x: 2, y: 2, z: 4, core: 2. Of those that a mesh axis runs over, the one named last changes fastest.
Arguments:
- latent: bfloat16 [16, 1, 3, 16, 128], P('wa', None, None, 'ha'), may hold values from -64 to 64
- conv_in_weight: bfloat16 [3, 3, 3, 16, 512], replicated, may hold values from -0.3125 to 0.3125
- conv_in_bias: float32 [512], replicated, may hold values from -3 to 3
- norm1_gain: float32 [512], replicated, may hold values from 0.5 to 1.5
- norm1_shift: float32 [512], replicated, may hold values from -3 to 3
- conv1_weight: bfloat16 [3, 3, 3, 512, 512], replicated, may hold values from -0.0546875 to 0.0546875
- conv1_bias: float32 [512], replicated, may hold values from -3 to 3
- norm2_gain: float32 [512], replicated, may hold values from 0.5 to 1.5
- norm2_shift: float32 [512], replicated, may hold values from -3 to 3
Outputs:
- decoded: bfloat16 [1, 3, 16, 128, 512], P(None, None, 'ha', 'wa')
All inputs are finite; a program needn't handle non-finite values.
Results may differ from a plain program's by a relative error of at most 0.0042.
Values may be sent and summed in bfloat16 or wider, within the bound.
A program may use at most 64 MiB of HBM per device.

v0:
```python
import jax
import jax.numpy as jnp
from jax import lax
from jax.sharding import PartitionSpec as P

GROUPS = 32


epsilon = 1e-06


def extended_2(value, sides, width):
    for axis, dim in sides:
        count, length = (lax.axis_size(axis), value.shape[dim])
        up = [(i, (i + 1) % count) for i in range(count - 1)]
        down = [(j, i) for i, j in up]
        last = lax.slice_in_dim(value, length - width, length, axis=dim)
        first = lax.slice_in_dim(value, 0, width, axis=dim)
        before = lax.ppermute(last, axis, up)
        after = lax.ppermute(first, axis, down)
        value = jnp.concatenate([before, value, after], axis=dim)
    return value


def causal_frames(values):
    first = values[:, :1]
    return jnp.concatenate([first, first, values], axis=1)


def fix_edges(extended, margin):
    at_top = lax.axis_index("ha") == 0
    at_bottom = lax.axis_index("ha") == lax.axis_size("ha") - 1
    total_rows = extended.shape[2]
    upper_rim = jnp.where(at_top, extended[:, :, margin : margin + 1], extended[:, :, :margin])
    lower_rim = jnp.where(
        at_bottom,
        extended[:, :, total_rows - margin - 1 : total_rows - margin],
        extended[:, :, total_rows - margin :],
    )
    extended = jnp.concatenate(
        [upper_rim, extended[:, :, margin : total_rows - margin], lower_rim], axis=2
    )
    at_left = lax.axis_index("wa") == 0
    at_right = lax.axis_index("wa") == lax.axis_size("wa") - 1
    total_cols = extended.shape[3]
    left_rim = jnp.where(
        at_left, extended[:, :, :, margin : margin + 1], extended[:, :, :, :margin]
    )
    right_rim = jnp.where(
        at_right,
        extended[:, :, :, total_cols - margin - 1 : total_cols - margin],
        extended[:, :, :, total_cols - margin :],
    )
    return jnp.concatenate(
        [left_rim, extended[:, :, :, margin : total_cols - margin], right_rim], axis=3
    )


def conv_valid(padded, weight):
    return lax.conv_general_dilated(
        padded,
        weight,
        (1, 1, 1),
        "VALID",
        dimension_numbers=("NDHWC", "DHWIO", "NDHWC"),
        preferred_element_type=jnp.float32,
    )


def group_stats(interior):
    batch_size = interior.shape[0]
    grouped = interior.reshape(batch_size, -1, GROUPS, interior.shape[-1] // GROUPS)
    cell_count = grouped.shape[1] * grouped.shape[3] * lax.axis_size("ha") * lax.axis_size("wa")
    totals = lax.psum(jnp.sum(grouped, axis=(1, 3)), ("ha", "wa"))
    group_mean = totals / cell_count
    centered = grouped - group_mean[:, None, :, None]
    spread = lax.psum(jnp.sum(centered * centered, axis=(1, 3)), ("ha", "wa"))
    variance = spread / cell_count
    return (group_mean, lax.rsqrt(variance + epsilon))


def group_activate(field, group_mean, inverse_std, norm_gain, norm_shift):
    batch_size = field.shape[0]
    grouped = field.reshape(batch_size, -1, GROUPS, field.shape[-1] // GROUPS)
    normed = (grouped - group_mean[:, None, :, None]) * inverse_std[:, None, :, None]
    return jax.nn.silu(normed.reshape(field.shape) * norm_gain + norm_shift)


def on_device(
    latent,
    conv_in_weight,
    conv_in_bias,
    norm1_gain,
    norm1_shift,
    conv1_weight,
    conv1_bias,
    norm2_gain,
    norm2_shift,
):
    tiled_latent = lax.all_to_all(latent, "wa", split_axis=4, concat_axis=0, tiled=True)
    tiled_latent = jnp.transpose(tiled_latent, (1, 2, 3, 4, 0))
    rim_width = 1
    latent_ext = extended_2(tiled_latent, (("ha", 2), ("wa", 3)), rim_width)
    latent_ext = fix_edges(latent_ext, rim_width)
    hidden = conv_valid(causal_frames(latent_ext), conv_in_weight) + conv_in_bias
    group_mean, inverse_std = group_stats(hidden)
    active = group_activate(hidden, group_mean, inverse_std, norm1_gain, norm1_shift).astype(
        jnp.bfloat16
    )
    active_rim = extended_2(active, (("ha", 2), ("wa", 3)), 1)
    active_rim = fix_edges(active_rim, 1)
    convolved = conv_valid(causal_frames(active_rim), conv1_weight) + conv1_bias
    second_mean, second_inverse = group_stats(convolved)
    return group_activate(convolved, second_mean, second_inverse, norm2_gain, norm2_shift).astype(
        jnp.bfloat16
    )


def solution(mesh):
    return jax.shard_map(
        on_device,
        mesh=mesh,
        in_specs=(P("wa", None, None, "ha", None), P(), P(), P(), P(), P(), P(), P(), P()),
        out_specs=P(None, None, "ha", "wa", None),
        check_vma=False,
    )
```

profile of v0, /device:TPU:0, one launch (start us, length us, event | category | flops | bytes accessed | tf_op | source)
XLA Modules:
  0.0 236.3 jit_solution(16982870794635283046)
XLA Ops:
  0.0 0.9 copy.19
  0.9 15.1 %all_to_all.18 = bf16[1,1,3,8,128]{3,2,1,0,4:T(4,128)(2,1)S(1)} all-to-all(bf16[1,1,3,8,128]{3,2,1,0,4:T(4,128)(2,1)S(1)} %copy.19), channel_id=1, replica_groups=mesh['ha'=2,'wa'=16] {'wa'}, dimensions={4} | all-to-all | bytes 12288 | tf_op jit(solution)/shard_map/all_to_all | solution.py:100
  16.0 0.2 copy.27
  16.3 3.4 %collective-permute-start = (bf16[1,3,1,8,16]{4,0,3,2,1:T(2,128)(2,1)S(1)}, bf16[1,3,1,8,16]{4,0,3,2,1:T(2,128)(2,1)S(1)}, u32[]{:S(2)}, u32[]{:S(2)}) collective-permute-start(bf16[1,3,1,8,16]{4,0,3,2,1:T(2,128)(2,1)S(1)} %get-tuple-element.15), channel_id=1, source_target_pairs={{0,16},{1,17},{2,18},{3,19},{4,20},{5,21},{6,22},{7,23},{8,24},{9,... | collective-permute-start | bytes 2312 | tf_op jit(solution)/shard_map/ppermute | solution.py:19
  19.7 1.3 collective-permute-start.1
  21.1 4.2 %collective-permute-done.1 = bf16[1,3,1,8,16]{4,0,3,2,1:T(2,128)(2,1)S(1)} collective-permute-done((bf16[1,3,1,8,16]{4,0,3,2,1:T(2,128)(2,1)S(1)}, bf16[1,3,1,8,16]{4,0,3,2,1:T(2,128)(2,1)S(1)}, u32[]{:S(2)}, u32[]{:S(2)}) %collective-permute-start.1) | collective-permute-done | bytes 800 | tf_op jit(solution)/shard_map/ppermute | solution.py:20
  25.4 1.3 collective-permute-start.2
  26.7 1.3 collective-permute-start.3
  28.0 1.8 collective-permute-done.3
  29.8 0.3 pad_maximum_fusion.4
  30.1 0.1 slice.122
  30.4 0.3 pad_maximum_fusion.5
  30.6 0.1 slice.123
  31.0 1.8 fusion.4
  33.0 0.1 reduce_sum.55
  33.2 41.8 %psum.28 = f32[1,32]{1,0:T(1,128)S(1)} all-reduce(f32[1,32]{1,0:T(1,128)S(1)} %bitcast.30), channel_id=1, replica_groups=mesh['ha'=2,'wa'=16] {'ha','wa'}, use_global_device_ids=true, to_apply=%region_2.3 | all-reduce | flops 32 | bytes 256 | tf_op jit(solution)/shard_map/psum | solution.py:74
  75.4 38.5 %psum.29 = f32[1,32]{1,0:T(1,128)S(1)} all-reduce(f32[1,32]{1,0:T(1,128)S(1)} %bitcast.31), channel_id=1, replica_groups=mesh['ha'=2,'wa'=16] {'ha','wa'}, use_global_device_ids=true, to_apply=%region_5.6 | all-reduce | flops 32 | bytes 256 | tf_op jit(solution)/shard_map/psum | solution.py:77
  114.1 0.1 multiply_convert_fusion.1
  114.2 4.2 %collective-permute-start.4 = (bf16[1,3,1,8,512]{4,3,2,1,0:T(8,128)(2,1)S(1)}, bf16[1,3,1,8,512]{4,3,2,1,0:T(8,128)(2,1)S(1)}, u32[]{:S(2)}, u32[]{:S(2)}) collective-permute-start(bf16[1,3,1,8,512]{4,3,2,1,0:T(8,128)(2,1)S(1)} %get-tuple-element.9), channel_id=1, source_target_pairs={{0,16},{1,17},{2,18},{3,19},{4,20},{5,21},{6,22},{7,23},{8,24},{9,... | collective-permute-start | bytes 73736 | tf_op jit(solution)/shard_map/ppermute | solution.py:19
  118.4 1.3 collective-permute-start.5
  119.7 0.2 collective-permute-done.4
  119.9 4.2 %collective-permute-done.5 = bf16[1,3,1,8,512]{4,3,2,1,0:T(8,128)(2,1)S(1)} collective-permute-done((bf16[1,3,1,8,512]{4,3,2,1,0:T(8,128)(2,1)S(1)}, bf16[1,3,1,8,512]{4,3,2,1,0:T(8,128)(2,1)S(1)}, u32[]{:S(2)}, u32[]{:S(2)}) %collective-permute-start.5) | collective-permute-done | bytes 24608 | tf_op jit(solution)/shard_map/ppermute | solution.py:20
  124.2 1.3 collective-permute-start.6
  125.5 1.5 collective-permute-start.7
  127.0 3.8 %collective-permute-done.7 = bf16[1,3,10,1,512]{4,3,2,1,0:T(2,128)(2,1)S(1)} collective-permute-done((bf16[1,3,10,1,512]{4,3,2,1,0:T(2,128)(2,1)S(1)}, bf16[1,3,10,1,512]{4,3,2,1,0:T(2,128)(2,1)S(1)}, u32[]{:S(2)}, u32[]{:S(2)}) %collective-permute-start.7) | collective-permute-done | bytes 30752 | tf_op jit(solution)/shard_map/ppermute | solution.py:20
  130.8 0.3 pad_maximum_fusion
  131.3 0.2 broadcast_select_fusion.1
  131.7 0.3 maximum_maximum_fusion
  132.1 21.8 %fusion = f32[1,3,8,8,512]{4,0,3,2,1:T(1,128)S(1)} fusion(bf16[3,3,3,512,512]{4,3,2,1,0:T(8,128)(2,1)} %param.14, bf16[1,5,10,10,512]{4,3,2,1,0:T(8,128)(2,1)S(1)} %maximum_maximum_fusion), kind=kOutput, calls=%fused_computation | convolution fusion | flops 2717908992 | bytes 15060992 | tf_op jit(solution)/shard_map/conv_general_dilated | solution.py:60
  154.2 41.5 %psum.30 = f32[1,32]{1,0:T(1,128)S(1)} all-reduce(f32[1,32]{1,0:T(1,128)S(1)} %bitcast.32), channel_id=1, replica_groups=mesh['ha'=2,'wa'=16] {'ha','wa'}, use_global_device_ids=true, to_apply=%region_8.9 | all-reduce | flops 32 | bytes 256 | tf_op jit(solution)/shard_map/psum | solution.py:74
  196.1 39.2 %psum.31 = f32[1,32]{1,0:T(1,128)S(1)} all-reduce(f32[1,32]{1,0:T(1,128)S(1)} %bitcast.29), channel_id=1, replica_groups=mesh['ha'=2,'wa'=16] {'ha','wa'}, use_global_device_ids=true, to_apply=%region_11.12 | all-reduce | flops 32 | bytes 256 | tf_op jit(solution)/shard_map/psum | solution.py:77
  235.5 0.8 multiply_convert_fusion
  (55 shorter events, 2.7 us)
Async XLA Ops:
  0.0 31.0 %copy-start = (bf16[3,3,3,16,512]{4,3,2,1,0:T(8,128)(2,1)S(1)}, bf16[3,3,3,16,512]{4,3,2,1,0:T(8,128)(2,1)}, u32[]{:S(2)}) copy-start(bf16[3,3,3,16,512]{4,3,2,1,0:T(8,128)(2,1)} %param.10) | copy-start | bytes 1327108
  16.3 4.8 %collective-permute-start = (bf16[1,3,1,8,16]{4,0,3,2,1:T(2,128)(2,1)S(1)}, bf16[1,3,1,8,16]{4,0,3,2,1:T(2,128)(2,1)S(1)}, u32[]{:S(2)}, u32[]{:S(2)}) collective-permute-start(bf16[1,3,1,8,16]{4,0,3,2,1:T(2,128)(2,1)S(1)} %get-tuple-element.15), channel_id=1, source_target_pairs={{0,16},{1,17},{2,18},{3,19},{4,20},{5,21},{6,22},{7,23},{8,24},{9,... | collective-permute-start | bytes 2312 | tf_op jit(solution)/shard_map/ppermute | solution.py:19
  19.7 5.6 %collective-permute-start.1 = (bf16[1,3,1,8,16]{4,0,3,2,1:T(2,128)(2,1)S(1)}, bf16[1,3,1,8,16]{4,0,3,2,1:T(2,128)(2,1)S(1)}, u32[]{:S(2)}, u32[]{:S(2)}) collective-permute-start(bf16[1,3,1,8,16]{4,0,3,2,1:T(2,128)(2,1)S(1)} %get-tuple-element.16), channel_id=1, source_target_pairs={{16,0},{17,1},{18,2},{19,3},{20,4},{21,5},{22,6},{23,7},{24,8},{25... | collective-permute-start | bytes 2312 | tf_op jit(solution)/shard_map/ppermute | solution.py:20
  25.4 2.6 %collective-permute-start.2 = (bf16[1,3,10,1,16]{4,0,3,2,1:T(2,128)(2,1)S(1)}, bf16[1,3,10,1,16]{4,0,3,2,1:T(2,128)(2,1)S(1)}, u32[]{:S(2)}, u32[]{:S(2)}) collective-permute-start(bf16[1,3,10,1,16]{4,0,3,2,1:T(2,128)(2,1)S(1)} %get-tuple-element.13), channel_id=1, source_target_pairs={{0,1},{1,2},{2,3},{3,4},{4,5},{5,6},{6,7},{7,8},{8,9},{9,10},{10,1... | collective-permute-start | bytes 2888 | tf_op jit(solution)/shard_map/ppermute | solution.py:19
  26.7 3.1 %collective-permute-start.3 = (bf16[1,3,10,1,16]{4,0,3,2,1:T(2,128)(2,1)S(1)}, bf16[1,3,10,1,16]{4,0,3,2,1:T(2,128)(2,1)S(1)}, u32[]{:S(2)}, u32[]{:S(2)}) collective-permute-start(bf16[1,3,10,1,16]{4,0,3,2,1:T(2,128)(2,1)S(1)} %get-tuple-element.14), channel_id=1, source_target_pairs={{1,0},{2,1},{3,2},{4,3},{5,4},{6,5},{7,6},{8,7},{9,8},{10,9},{11,1... | collective-permute-start | bytes 2888 | tf_op jit(solution)/shard_map/ppermute | solution.py:20
  31.0 1.9 copy-start.1
  31.0 83.0 %copy-start.3 = (f32[512]{0:T(512)S(1)}, f32[512]{0:T(512)}, u32[]{:S(2)}) copy-start(f32[512]{0:T(512)} %param.13) | copy-start | bytes 6148
  31.0 83.0 %copy-start.4 = (f32[512]{0:T(512)S(1)}, f32[512]{0:T(512)}, u32[]{:S(2)}) copy-start(f32[512]{0:T(512)} %param.12) | copy-start | bytes 6148
  114.2 5.7 %collective-permute-start.4 = (bf16[1,3,1,8,512]{4,3,2,1,0:T(8,128)(2,1)S(1)}, bf16[1,3,1,8,512]{4,3,2,1,0:T(8,128)(2,1)S(1)}, u32[]{:S(2)}, u32[]{:S(2)}) collective-permute-start(bf16[1,3,1,8,512]{4,3,2,1,0:T(8,128)(2,1)S(1)} %get-tuple-element.9), channel_id=1, source_target_pairs={{0,16},{1,17},{2,18},{3,19},{4,20},{5,21},{6,22},{7,23},{8,24},{9,... | collective-permute-start | bytes 73736 | tf_op jit(solution)/shard_map/ppermute | solution.py:19
  118.4 5.7 %collective-permute-start.5 = (bf16[1,3,1,8,512]{4,3,2,1,0:T(8,128)(2,1)S(1)}, bf16[1,3,1,8,512]{4,3,2,1,0:T(8,128)(2,1)S(1)}, u32[]{:S(2)}, u32[]{:S(2)}) collective-permute-start(bf16[1,3,1,8,512]{4,3,2,1,0:T(8,128)(2,1)S(1)} %get-tuple-element.10), channel_id=1, source_target_pairs={{16,0},{17,1},{18,2},{19,3},{20,4},{21,5},{22,6},{23,7},{24,8},{25... | collective-permute-start | bytes 73736 | tf_op jit(solution)/shard_map/ppermute | solution.py:20
  124.2 2.8 %collective-permute-start.6 = (bf16[1,3,10,1,512]{4,3,2,1,0:T(2,128)(2,1)S(1)}, bf16[1,3,10,1,512]{4,3,2,1,0:T(2,128)(2,1)S(1)}, u32[]{:S(2)}, u32[]{:S(2)}) collective-permute-start(bf16[1,3,10,1,512]{4,3,2,1,0:T(2,128)(2,1)S(1)} %get-tuple-element.7), channel_id=1, source_target_pairs={{0,1},{1,2},{2,3},{3,4},{4,5},{5,6},{6,7},{7,8},{8,9},{9,10},{10,1... | collective-permute-start | bytes 92168 | tf_op jit(solution)/shard_map/ppermute | solution.py:19
  125.5 5.3 %collective-permute-start.7 = (bf16[1,3,10,1,512]{4,3,2,1,0:T(2,128)(2,1)S(1)}, bf16[1,3,10,1,512]{4,3,2,1,0:T(2,128)(2,1)S(1)}, u32[]{:S(2)}, u32[]{:S(2)}) collective-permute-start(bf16[1,3,10,1,512]{4,3,2,1,0:T(2,128)(2,1)S(1)} %get-tuple-element.8), channel_id=1, source_target_pairs={{1,0},{2,1},{3,2},{4,3},{5,4},{6,5},{7,6},{8,7},{9,8},{10,9},{11,1... | collective-permute-start | bytes 92168 | tf_op jit(solution)/shard_map/ppermute | solution.py:20
  132.1 21.8 %copy-start.2 = (f32[512]{0:T(512)S(1)}, f32[512]{0:T(512)}, u32[]{:S(2)}) copy-start(f32[512]{0:T(512)} %param.15) | copy-start | bytes 6148
  132.1 103.4 %copy-start.5 = (f32[512]{0:T(512)S(1)}, f32[512]{0:T(512)}, u32[]{:S(2)}) copy-start(f32[512]{0:T(512)} %param.17) | copy-start | bytes 6148
  132.1 103.4 %copy-start.6 = (f32[512]{0:T(512)S(1)}, f32[512]{0:T(512)}, u32[]{:S(2)}) copy-start(f32[512]{0:T(512)} %param.16) | copy-start | bytes 6148
where the time goes:
time: 237 us; the launch traced here: 236 us
  blocking collectives  176 us (74%)
  matrix products  23.6 us (10%)
  starting transfers between devices  15.5 us (7%)
  waiting for transfers between devices  14.3 us (6%)
  other arithmetic  3.85 us (2%)
  local copies, waits for them, and re-layouts  2.53 us (1%)
    psum x2, blocking collectives, group_stats(): totals = lax.psum(jnp.sum(grouped, axis=(1, 3)), ('ha', 'wa'))  83.3 us
    psum x2, blocking collectives, group_stats(): spread = lax.psum(jnp.sum(centered * centered, axis=(1, 3)), ('ha', 'wa'))  77.7 us
    conv_general_dilated x2, matrix products, conv_valid(): lax.conv_general_dilated(padded, weight, (1, 1, 1), 'VALID', dimension_nu...  23.6 us
    all_to_all x1, blocking collectives, on_device(): lax.all_to_all(latent, 'wa', split_axis=4, concat_axis=0, tiled=True)  15.1 us
    ppermute x4, waiting for transfers between devices, extended_2(): after = lax.ppermute(first, axis, down)  14 us
    ppermute x4, starting transfers between devices, extended_2(): before = lax.ppermute(last, axis, up)  10.2 us
    ppermute x4, starting transfers between devices, extended_2(): after = lax.ppermute(first, axis, down)  5.35 us
  transfers between devices with their start and end apart: 8, of which 6 were waited for; matrix products, arithmetic and copies ran while one was open for 0% of the time, Pallas kernels for 0%

commit v1 on v0

v1 whole, which is shorter than its diff:
```python
import functools

import jax
import jax.numpy as jnp
from jax import lax
from jax.experimental import pallas as pl
from jax.experimental.pallas import tpu as pltpu
from jax.sharding import PartitionSpec as P

GROUPS = 32
EPSILON = 1e-06
MESH = pl.DeviceIdType.MESH
LANES = 128
CELL = 16


def lanes_of(rows):
    return lax.broadcasted_iota(jnp.int32, (rows, LANES), 1)


def group_sum(x):
    lane = lanes_of(x.shape[0])
    for s in (1, 2, 4, 8):
        x = x + jnp.where((lane & s) == 0, pltpu.roll(x, LANES - s, 1), pltpu.roll(x, s, 1))
    return x


def to_rows(x):
    return jnp.concatenate([x[:, k * LANES : (k + 1) * LANES] for k in range(4)], axis=0)


def to_lanes(x):
    return jnp.concatenate([x[k : k + 1] for k in range(4)], axis=1)


def pack_stats(total, spread):
    sub = lanes_of(1) & 15
    row = jnp.zeros((1, LANES), jnp.float32)
    for k in range(4):
        row = jnp.where(sub == k, total[k : k + 1], row)
        row = jnp.where(sub == 4 + k, spread[k : k + 1], row)
    return row


def unpack_stats(mean, inverse):
    sub = lanes_of(1) & 15
    rows = [jnp.where(sub == k, mean, 0.0) for k in range(4)]
    rows += [jnp.where(sub == k, inverse, 0.0) for k in range(4)]
    both = group_sum(jnp.concatenate(rows, axis=0))
    return to_lanes(both[:4]), to_lanes(both[4:])


def wait_bytes(ref, sem):
    pltpu.make_async_copy(ref, ref, sem).wait()


def kernel(
    ha,
    wa,
    lat_hbm,
    win_hbm,
    bin_hbm,
    g1_hbm,
    s1_hbm,
    w1_hbm,
    b1_hbm,
    g2_hbm,
    s2_hbm,
    out_ref,
    lat,
    win,
    vec,
    w1,
    pack,
    grid,
    hid,
    cols,
    conv,
    st_send,
    st_recv,
    local_sem,
    win_sem,
    w1_sem,
    lat_send,
    lat_recv,
    stat_send,
    stat_recv,
):
    h, w = lax.axis_index("ha"), lax.axis_index("wa")
    peers = ha * wa - 1

    def peer_of(dh, dw):
        ph, pw = h + dh, w + dw
        return (jnp.where(ph >= ha, ph - ha, ph), jnp.where(pw >= wa, pw - wa, pw))

    @pl.when(h == 0)
    def _():
        grid[0] = jnp.zeros((wa, 3, LANES), jnp.float32)

    @pl.when(h == ha - 1)
    def _():
        grid[2] = jnp.zeros((wa, 3, LANES), jnp.float32)

    lat_copy = pltpu.make_async_copy(lat_hbm, lat, local_sem.at[0])
    lat_copy.start()
    barrier = pltpu.get_barrier_semaphore()
    for dh in range(ha):
        for dw in range(wa):
            if dh or dw:
                pl.semaphore_signal(barrier, inc=1, device_id=peer_of(dh, dw), device_id_type=MESH)
    win_copies = []
    for kt in range(3):
        copy = pltpu.make_async_copy(win_hbm.at[kt], win.at[kt, pl.ds(0, 144)], win_sem.at[kt])
        copy.start()
        win_copies.append(copy)
    vec_copies = []
    for n, source in enumerate((bin_hbm, g1_hbm, s1_hbm, b1_hbm, g2_hbm, s2_hbm)):
        copy = pltpu.make_async_copy(source, vec.at[n], local_sem.at[2 + n])
        copy.start()
        vec_copies.append(copy)
    w1_copies = []
    for kt in range(3):
        copy = pltpu.make_async_copy(w1_hbm.at[kt], w1.at[kt], w1_sem.at[kt])
        copy.start()
        w1_copies.append(copy)

    win[:, 144:, :] = jnp.zeros((3, 112, 512), jnp.bfloat16)

    lat_copy.wait()
    tile = LANES // wa
    lane8 = lanes_of(8)
    row8 = lax.broadcasted_iota(jnp.int32, (8, LANES), 0)
    frames = []
    for t in range(3):
        x = lat[t].astype(jnp.float32)
        frames.append(pltpu.roll(x, 2, 1, stride=CELL, stride_axis=0))
    for dst in range(wa):
        for t in range(3):
            x = pltpu.roll(frames[t], (LANES - tile * dst) % LANES, 1) if dst else frames[t]
            x = jnp.where(lane8 // CELL == row8, x, 0.0)
            pack[dst, t : t + 1, :] = jnp.sum(x, axis=0, keepdims=True)

    pl.semaphore_wait(barrier, peers)

    def send_latent(dh, dw):
        pw = w + dw
        pw = jnp.where(pw >= wa, pw - wa, pw)
        pltpu.make_async_remote_copy(
            src_ref=pack.at[pw],
            dst_ref=grid.at[1 - dh, w],
            send_sem=lat_send.at[1 - dh],
            recv_sem=lat_recv.at[1 - dh],
            device_id=(h + dh, pw),
            device_id_type=MESH,
        ).start()

    pltpu.make_async_copy(pack.at[w], grid.at[1, w], lat_recv.at[1]).start()
    for dw in range(1, wa):
        send_latent(0, dw)

    @pl.when(h > 0)
    def _():
        for dw in range(wa):
            send_latent(-1, dw)

    @pl.when(h < ha - 1)
    def _():
        for dw in range(wa):
            send_latent(1, dw)

    wait_bytes(grid.at[1], lat_recv.at[1])

    @pl.when(h > 0)
    def _():
        wait_bytes(grid.at[0], lat_recv.at[0])

    @pl.when(h < ha - 1)
    def _():
        wait_bytes(grid.at[2], lat_recv.at[2])

    top, bottom = h == 0, h == ha - 1
    left_lane = jnp.where(w == 0, 1, -1)
    right_lane = jnp.where(w == wa - 1, tile + 2, -1)
    lane = lanes_of(wa)
    patches = []
    for t in range(3):
        up, own, down = (grid[s, :, t, :] for s in range(3))
        up = jnp.where(top, pltpu.roll(own, 16, 1), pltpu.roll(up, 32, 1))
        down = jnp.where(bottom, pltpu.roll(own, 48, 1), pltpu.roll(down, 32, 1))
        own = pltpu.roll(own, 32, 1)
        strips = [jnp.where(lane < 32, up, own), jnp.where(lane < 32, own, down)]
        for n in range(2):
            x = strips[n]
            x = jnp.where((lane & 15) == left_lane, pltpu.roll(x, LANES - 1, 1), x)
            strips[n] = jnp.where((lane & 15) == right_lane, pltpu.roll(x, 1, 1), x)
        first, second = strips
        pieces = []
        for ki in range(3):
            for kj in range(3):
                s = ki * CELL + kj
                if s:
                    a, b = pltpu.roll(first, LANES - s, 1), pltpu.roll(second, LANES - s, 1)
                    a = jnp.where(lane < LANES - s, a, b)
                else:
                    a, b = first, second
                pieces.append((a, b))
        pieces.append((jnp.zeros((112, LANES), jnp.float32),) * 2)
        a = jnp.concatenate([p[0] for p in pieces], axis=0).T
        b = jnp.concatenate([p[1] for p in pieces], axis=0).T
        patches.append(jnp.concatenate([a, b[:32]], axis=0).astype(jnp.bfloat16))

    for copy in win_copies + vec_copies:
        copy.wait()

    def product(t, kt):
        return jnp.dot(patches[t], win[kt], preferred_element_type=jnp.float32)

    d00 = product(0, 0) + vec[0]
    d01 = d00 + product(0, 1)
    hid[0] = d01 + product(0, 2)
    hid[1] = d01 + product(1, 2)
    hid[2] = d00 + product(1, 1) + product(2, 2)

    group_cells = 3 * 64 * 16
    all_cells = group_cells * ha * wa
    position = lax.broadcasted_iota(jnp.int32, (160, LANES), 0)
    cell_i, cell_j = position // CELL, position & 15
    inside = (cell_i >= 1) & (cell_i <= 8) & (cell_j >= 1) & (cell_j <= 8)

    def exchange(phase, total, spread):
        mine = pack_stats(total, spread)
        st_send[phase] = mine
        for dh in range(ha):
            for dw in range(wa):
                if dh or dw:
                    pltpu.make_async_remote_copy(
                        src_ref=st_send.at[phase],
                        dst_ref=st_recv.at[phase, dh * wa + dw - 1],
                        send_sem=stat_send.at[phase],
                        recv_sem=stat_recv.at[phase],
                        device_id=peer_of(dh, dw),
                        device_id_type=MESH,
                    ).start()
        wait_bytes(st_recv.at[phase], stat_recv.at[phase])
        theirs = st_recv[phase]
        totals = jnp.sum(theirs, axis=0) + mine
        mean = totals / all_cells
        off = theirs * (1.0 / group_cells) - mean[None]
        off_mine = mine * (1.0 / group_cells) - mean
        between = jnp.sum(off * off, axis=0) + off_mine * off_mine
        spread_all = pltpu.roll(totals, LANES - 4, 1) + between * group_cells
        return unpack_stats(mean, lax.rsqrt(spread_all / all_cells + EPSILON))

    def statistics(blocks):
        sums = []
        for k in range(4):
            sums.append(sum(jnp.sum(b, axis=0, keepdims=True) for b in blocks(k)))
        total = group_sum(jnp.concatenate(sums, axis=0))
        mean = total / group_cells
        spreads = []
        for k in range(4):
            spreads.append(
                sum(jnp.sum(b, axis=0, keepdims=True) for b in blocks(k, mean[k : k + 1]))
            )
        return total, group_sum(jnp.concatenate(spreads, axis=0))

    def hidden_blocks(k, mean=None):
        for t in range(3):
            x = hid[t, :, k * LANES : (k + 1) * LANES]
            if mean is not None:
                x = (x - mean) * (x - mean)
            yield jnp.where(inside, x, 0.0)

    mean, inverse = exchange(0, *statistics(hidden_blocks))
    scale = inverse * vec[1]
    shift = vec[2]

    for copy in w1_copies:
        copy.wait()
    left_row = jnp.where(w == 0, 0, -1)
    right_row = jnp.where(w == wa - 1, 7, -1)
    row = lax.broadcasted_iota(jnp.int32, (10, 8, LANES), 1)
    for t in range(3):
        for k in range(4):
            part = slice(k * LANES, (k + 1) * LANES)
            x = hid[t, :, part]
            x = (x - mean[:, part]) * scale[:, part] + shift[:, part]
            x = (0.5 * x * (1.0 + jnp.tanh(0.5 * x))).reshape(10, 16, LANES)
            middle = x[:, 1:9]
            shifted = [
                jnp.where(row == left_row, middle, x[:, 0:8]),
                middle,
                jnp.where(row == right_row, middle, x[:, 2:10]),
            ]
            for kj in range(3):
                y = shifted[kj]
                y = jnp.concatenate(
                    [
                        jnp.where(top, y[1:2], y[0:1]),
                        y[1:9],
                        jnp.where(bottom, y[8:9], y[9:10]),
                    ],
                    axis=0,
                )
                for ki in range(3):
                    at = (ki * 3 + kj) * 512 + k * LANES
                    cols[t * 64 : (t + 1) * 64, at : at + LANES] = (
                        y[ki : ki + 8].reshape(64, LANES).astype(jnp.bfloat16)
                    )

    def conv_part(kt):
        total = 0.0
        for n in range(9):
            at = slice(n * 512, (n + 1) * 512)
            total += jnp.dot(cols[: 64 * (kt + 1), at], w1[kt, at], preferred_element_type=jnp.float32)
        return total

    c0 = conv_part(0) + vec[3]
    c1 = conv_part(1)
    c01 = c0 + c1[:64]
    c2 = conv_part(2)
    conv[0:64] = c01 + c2[:64]
    conv[64:128] = c01 + c2[64:128]
    conv[128:192] = c0 + c1[64:] + c2[128:]

    def conv_blocks(k, mean=None):
        x = conv[:, k * LANES : (k + 1) * LANES]
        if mean is not None:
            x = (x - mean) * (x - mean)
        yield x

    mean, inverse = exchange(1, *statistics(conv_blocks))
    scale = inverse * vec[4]
    shift = vec[5]
    for k in range(4):
        part = slice(k * LANES, (k + 1) * LANES)
        x = (conv[:, part] - mean[:, part]) * scale[:, part] + shift[:, part]
        out_ref[:, part] = (0.5 * x * (1.0 + jnp.tanh(0.5 * x))).astype(out_ref.dtype)

    wait_bytes(pack.at[pl.ds(0, wa - 1)], lat_send.at[1])

    @pl.when(h > 0)
    def _():
        wait_bytes(pack, lat_send.at[2])

    @pl.when(h < ha - 1)
    def _():
        wait_bytes(pack, lat_send.at[0])

    for phase in range(2):
        wait_bytes(st_recv.at[phase], stat_send.at[phase])


def on_device(ha, wa, latent, w_in, b_in, g1, s1, w1, b1, g2, s2):
    peers = ha * wa - 1
    vectors = [v.reshape(1, 512) for v in (b_in, g1, s1, b1, g2, s2)]
    out = pl.pallas_call(
        functools.partial(kernel, ha, wa),
        out_shape=jax.ShapeDtypeStruct((192, 512), jnp.bfloat16),
        in_specs=[pl.BlockSpec(memory_space=pl.ANY)] * 9,
        out_specs=pl.BlockSpec(memory_space=pltpu.VMEM),
        scratch_shapes=[
            pltpu.VMEM((3, 8, LANES), jnp.bfloat16),
            pltpu.VMEM((3, 256, 512), jnp.bfloat16),
            pltpu.VMEM((6, 1, 512), jnp.float32),
            pltpu.VMEM((3, 4608, 512), jnp.bfloat16),
            pltpu.VMEM((wa, 3, LANES), jnp.float32),
            pltpu.VMEM((3, wa, 3, LANES), jnp.float32),
            pltpu.VMEM((3, 160, 512), jnp.float32),
            pltpu.VMEM((192, 4608), jnp.bfloat16),
            pltpu.VMEM((192, 512), jnp.float32),
            pltpu.VMEM((2, 1, LANES), jnp.float32),
            pltpu.VMEM((2, peers, 1, LANES), jnp.float32),
            pltpu.SemaphoreType.DMA((8,)),
            pltpu.SemaphoreType.DMA((3,)),
            pltpu.SemaphoreType.DMA((3,)),
            pltpu.SemaphoreType.DMA((3,)),
            pltpu.SemaphoreType.DMA((3,)),
            pltpu.SemaphoreType.DMA((2,)),
            pltpu.SemaphoreType.DMA((2,)),
        ],
        compiler_params=pltpu.CompilerParams(
            collective_id=0, has_side_effects=True, vmem_limit_bytes=56 * 1024 * 1024
        ),
    )(
        latent.reshape(3, 8, LANES),
        w_in.reshape(3, 144, 512),
        vectors[0],
        vectors[1],
        vectors[2],
        w1.reshape(3, 4608, 512),
        vectors[3],
        vectors[4],
        vectors[5],
    )
    return out.reshape(1, 3, 8, 8, 512)


def solution(mesh):
    return jax.shard_map(
        functools.partial(on_device, mesh.shape["ha"], mesh.shape["wa"]),
        mesh=mesh,
        in_specs=(P("wa", None, None, "ha", None), P(), P(), P(), P(), P(), P(), P(), P()),
        out_specs=P(None, None, "ha", "wa", None),
        check_vma=False,
    )
```

time: 237 us -> 27.1 us (0.11)
  blocking collectives: 176 us -> 0 us
  Pallas kernels: 0 us -> 25.3 us
  matrix products: 23.6 us -> 0 us
  starting transfers between devices: 15.5 us -> 0 us
  waiting for transfers between devices: 14.3 us -> 0 us
  other arithmetic: 3.85 us -> 0 us
    psum x4 -> x0, blocking collectives: 161 us -> none  [the longest x2 83.3 us: group_stats(): totals = lax.psum(jnp.sum(grouped, axis=(1, 3)), ('ha', 'wa'))]
    pallas_call x0 -> x1, Pallas kernels: none -> 25.3 us  [on_device(): pl.pallas_call(functools.partial(kernel, ha, wa), out_shape=jax.ShapeDtyp...]
    conv_general_dilated x2 -> x0, matrix products: 23.6 us -> none  [conv_valid(): lax.conv_general_dilated(padded, weight, (1, 1, 1), 'VALID', dimension_nu...]
    ppermute x8 -> x0, starting transfers between devices: 15.5 us -> none  [the longest x4 10.2 us: extended_2(): before = lax.ppermute(last, axis, up)]
    all_to_all x1 -> x0, blocking collectives: 15.1 us -> none  [on_device(): lax.all_to_all(latent, 'wa', split_axis=4, concat_axis=0, tiled=True)]
    ppermute x8 -> x0, waiting for transfers between devices: 14.3 us -> none  [the longest x4 14 us: extended_2(): after = lax.ppermute(first, axis, down)]
  transfers between devices with their start and end apart: 8 -> 0, of which waited for: 6 -> 0; matrix products, arithmetic and copies ran while one was open for 0% -> 0% of each run, Pallas kernels for 0% -> 0%
where the time goes in v1:
time: 27.1 us; the launch traced here: 26.9 us
  Pallas kernels  25.3 us (93%)
  local copies, waits for them, and re-layouts  1.62 us (6%)
    pallas_call x1, Pallas kernels, on_device(): pl.pallas_call(functools.partial(kernel, ha, wa), out_shape=jax.ShapeDtyp...  25.3 us
    unnamed x1, local copies, waits for them, and re-layouts  1.62 us

profile of v1, /device:TPU:0, one launch (start us, length us, event | category | flops | bytes accessed | tf_op | source)
XLA Modules:
  0.0 26.9 jit_solution(9761728478439025681)
XLA Ops:
  0.0 25.3 %shard_map.91 = bf16[192,512]{1,0:T(8,128)(2,1)} custom-call(bf16[3,8,128]{2,1,0:T(8,128)(2,1)} %bitcast.13, bf16[3,144,512]{2,1,0:T(8,128)(2,1)} %bitcast.12, f32[1,512]{1,0:T(1,128)} %bitcast.14, f32[1,512]{1,0:T(1,128)} %bitcast.15, f32[1,512]{1,0:T(1,128)} %bitcast.16, bf16[3,4608,512]{2,1,0:T(8,128)(2,1)} %bitcast.10, f32[1,512]{1,0:T(1,128)} %bitcast.17, ...), custom_call_target="tpu_custom_call" | custom-call | tf_op jit(solution)/shard_map/pallas_call | solution.py:357
  25.3 1.6 %copy.11 = bf16[1,3,8,8,512]{4,3,2,1,0:T(8,128)(2,1)} copy(bf16[1,3,8,8,512]{4,3,2,1,0:T(8,128)(2,1)} %bitcast.11) | data formatting | bytes 393216

commit v2 on v1

--- a/solution.py
+++ b/solution.py
@@ -308,20 +308,24 @@
                         y[ki : ki + 8].reshape(64, LANES).astype(jnp.bfloat16)
                     )
 
-    def conv_part(kt):
+    def conv_part(kt, part):
         total = 0.0
         for n in range(9):
             at = slice(n * 512, (n + 1) * 512)
-            total += jnp.dot(cols[: 64 * (kt + 1), at], w1[kt, at], preferred_element_type=jnp.float32)
+            total += jnp.dot(
+                cols[: 64 * (kt + 1), at], w1[kt, at, part], preferred_element_type=jnp.float32
+            )
         return total
 
-    c0 = conv_part(0) + vec[3]
-    c1 = conv_part(1)
-    c01 = c0 + c1[:64]
-    c2 = conv_part(2)
-    conv[0:64] = c01 + c2[:64]
-    conv[64:128] = c01 + c2[64:128]
-    conv[128:192] = c0 + c1[64:] + c2[128:]
+    for n in range(2):
+        part = slice(n * 256, (n + 1) * 256)
+        c0 = conv_part(0, part) + vec[3, :, part]
+        c1 = conv_part(1, part)
+        c01 = c0 + c1[:64]
+        c2 = conv_part(2, part)
+        conv[0:64, part] = c01 + c2[:64]
+        conv[64:128, part] = c01 + c2[64:128]
+        conv[128:192, part] = c0 + c1[64:] + c2[128:]
 
     def conv_blocks(k, mean=None):
         x = conv[:, k * LANES : (k + 1) * LANES]

time: 27.1 us -> 27.2 us (level)
  no operation moved by 1% of the time
where the time goes in v2:
time: 27.2 us; the launch traced here: 27 us
  Pallas kernels  25.4 us (93%)
  local copies, waits for them, and re-layouts  1.62 us (6%)
    pallas_call x1, Pallas kernels, on_device(): pl.pallas_call(functools.partial(kernel, ha, wa), out_shape=jax.ShapeDtyp...  25.4 us
    unnamed x1, local copies, waits for them, and re-layouts  1.62 us

profile of v2, /device:TPU:0, one launch (start us, length us, event | category | flops | bytes accessed | tf_op | source)
XLA Modules:
  0.0 27.0 jit_solution(10328792170409801865)
XLA Ops:
  0.0 25.4 %shard_map.91 = bf16[192,512]{1,0:T(8,128)(2,1)} custom-call(bf16[3,8,128]{2,1,0:T(8,128)(2,1)} %bitcast.13, bf16[3,144,512]{2,1,0:T(8,128)(2,1)} %bitcast.12, f32[1,512]{1,0:T(1,128)} %bitcast.14, f32[1,512]{1,0:T(1,128)} %bitcast.15, f32[1,512]{1,0:T(1,128)} %bitcast.16, bf16[3,4608,512]{2,1,0:T(8,128)(2,1)} %bitcast.10, f32[1,512]{1,0:T(1,128)} %bitcast.17, ...), custom_call_target="tpu_custom_call" | custom-call | tf_op jit(solution)/shard_map/pallas_call | solution.py:361
  25.4 1.6 %copy.11 = bf16[1,3,8,8,512]{4,3,2,1,0:T(8,128)(2,1)} copy(bf16[1,3,8,8,512]{4,3,2,1,0:T(8,128)(2,1)} %bitcast.11) | data formatting | bytes 393216
